TPU v7x, 256 devices: a whole 4x4x8 slice. The times are simulated.
256 devices in a mesh: branch: 2 (over x_hi), row: 16 (over z, x_lo), col: 8 (over y, core).
Axes of the slice: x: 4 (x_hi: 2, x_lo: 2; x = x_hi * 2 + x_lo), y: 4, z: 8, core: 2. Of those that a mesh axis runs over, the one named last changes fastest.
Arguments:
- queries: bfloat16 [2, 12288, 2048], P('branch', ('row', 'col')), may hold values from -6 to 6
- keys: bfloat16 [2, 12288, 2048], P('branch', ('row', 'col')), may hold values from -6 to 6
- values: bfloat16 [2, 12288, 2048], P('branch', ('row', 'col')), may hold values from -6 to 6
- text_keys: bfloat16 [2, 256, 2048], P('branch'), may hold values from -8 to 8
- text_values: bfloat16 [2, 256, 2048], P('branch'), may hold values from -6 to 6
- text_lengths: int32 [2], P('branch'), may hold values from 1 to 256, as said below
- step_index: int32 [1], replicated, may hold values from 40 to 49
- out_proj: bfloat16 [2048, 64], replicated, may hold values from -0.125 to 0.125
- latent: float32 [6, 128, 64, 16], P(None, 'row', 'col'), may hold values from -6 to 6
- conv_in_w: bfloat16 [3, 3, 3, 16, 512], replicated, may hold values from -0.3125 to 0.3125
- conv_in_b: float32 [512], replicated, may hold values from -1.5 to 1.5
- conv_mid_w: bfloat16 [3, 3, 3, 512, 512], P(None, None, None, None, 'branch'), may hold values from -0.0546875 to 0.0546875
- conv_mid_b: float32 [512], P('branch'), may hold values from -1.5 to 1.5
Outputs:
- guided: float32 [6, 128, 64, 16], P(None, 'row', 'col')
- decoded: float32 [6, 128, 64, 512], P(None, 'row', 'col', 'branch')
Inputs may be any that keep to these rules, and one draw needn't show every extreme that they name: `text_lengths`: one of the two branches has the full 256 text tokens.
All inputs are finite; a program needn't handle non-finite values.
Results may differ from a plain program's by a relative error of at most 0.0054.
Values may be sent and summed in bfloat16 or wider, within the bound.
A program may use at most 128 MiB of HBM per device.

v0:
```python
import jax
import jax.numpy as jnp
from jax import lax
from jax.sharding import PartitionSpec as P

HD = 128


NEG_FILL = -1e30
GUIDE_SCALE = 6.0


def from_partner(block, axis, apart):
    count = lax.axis_size(axis)
    route = []
    for low in range(count):
        high = low | 1 << apart
        if high != low and high < count:
            route += [(low, high), (high, low)]
    return lax.ppermute(block, axis, route)


def with_halo(cells, sides, width):
    for axis, dim in sides:
        count = lax.axis_size(axis)
        ends = count - 1
        head = lax.slice_in_dim(cells, 0, width, axis=dim)
        tail = lax.slice_in_dim(cells, cells.shape[dim] - width, cells.shape[dim], axis=dim)
        cells = jnp.concatenate(
            [
                lax.ppermute(tail, axis, [(i, (i + 1) % count) for i in range(ends)]),
                cells,
                lax.ppermute(head, axis, [((i + 1) % count, i) for i in range(ends)]),
            ],
            axis=dim,
        )
    return cells


def sigma_at(index):
    s = 1.0 - index.astype(jnp.float32) / 50.0
    return 7.0 * s / (1.0 + 6.0 * s)


def block_length(row_count):
    length = min(row_count, 1024)
    while row_count % length != 0:
        length = length - 1
    return length


def absorb(state_now, query_block, key_block, value_block, usable, score_scale):
    running_max, running_sum, weighted = state_now
    scores = (
        jnp.einsum("qhe,khe->qhk", query_block, key_block, preferred_element_type=jnp.float32)
        * score_scale
    )
    if usable is not None:
        scores = jnp.where(usable[None, None, :], scores, NEG_FILL)
    new_max = jnp.maximum(running_max, jnp.max(scores, axis=2))
    expo = jnp.exp(scores - new_max[..., None])
    if usable is not None:
        expo = jnp.where(usable[None, None, :], expo, 0.0)
    factor = jnp.exp(running_max - new_max)
    running_sum = running_sum * factor + jnp.sum(expo, axis=2)
    weighted = weighted * factor[..., None] + jnp.einsum(
        "qhk,khe->qhe", expo.astype(jnp.bfloat16), value_block, preferred_element_type=jnp.float32
    )
    return (new_max, running_sum, weighted)


def text_state(query_block, text_k, text_v, text_count, head_first, score_scale):
    head_count = query_block.shape[1]
    own_keys = lax.dynamic_slice_in_dim(text_k, head_first, head_count, 1)
    own_values = lax.dynamic_slice_in_dim(text_v, head_first, head_count, 1)
    usable = jnp.arange(text_k.shape[0]) < text_count
    empty = (
        jnp.full(query_block.shape[:2], NEG_FILL, jnp.float32),
        jnp.zeros(query_block.shape[:2], jnp.float32),
        jnp.zeros(query_block.shape, jnp.float32),
    )
    return absorb(empty, query_block, own_keys, own_values, usable, score_scale)


def key_folder(query_block, score_scale, state_now, key_piece):
    piece_keys, piece_values = key_piece
    row_count = piece_keys.shape[0]
    length = block_length(row_count)
    shaped_keys = piece_keys.reshape((row_count // length, length) + piece_keys.shape[1:])
    shaped_values = piece_values.reshape((row_count // length, length) + piece_values.shape[1:])

    def advance_block(inner, kv_pair):
        return (absorb(inner, query_block, kv_pair[0], kv_pair[1], None, score_scale), None)

    result, _ = lax.scan(advance_block, state_now, (shaped_keys, shaped_values))
    return result


def projector(attn_out, out_proj, head_first):
    span = attn_out.shape[1] * attn_out.shape[2]
    proj_rows = lax.dynamic_slice_in_dim(out_proj, head_first * attn_out.shape[2], span, 0)
    flattened = attn_out.reshape(attn_out.shape[0], span)
    return jnp.dot(flattened, proj_rows, preferred_element_type=jnp.float32)


def finish(state_now):
    running_max, running_sum, weighted = state_now
    return (weighted / running_sum[..., None]).astype(jnp.bfloat16)


def conv_taps(padded, weight, frame_count, row_count, col_count):
    result = jnp.zeros((frame_count * row_count * col_count, weight.shape[4]), jnp.float32)
    for tap_t in range(3):
        for tap_h in range(3):
            for tap_w in range(3):
                window = padded[
                    tap_t : tap_t + frame_count,
                    tap_h : tap_h + row_count,
                    tap_w : tap_w + col_count,
                ]
                result = result + jnp.dot(
                    window.reshape(-1, window.shape[3]),
                    weight[tap_t, tap_h, tap_w],
                    preferred_element_type=jnp.float32,
                )
    return result.reshape(frame_count, row_count, col_count, weight.shape[4])


def local(
    queries,
    keys,
    values,
    text_keys,
    text_values,
    text_lengths,
    step_index,
    out_proj,
    latent,
    conv_in_w,
    conv_in_b,
    conv_mid_w,
    conv_mid_b,
):
    tok_count = queries.shape[1]
    head_count = queries.shape[2] // HD
    score_scale = HD ** (-0.5)
    local_q = queries[0].reshape(tok_count, head_count, HD)
    local_k = keys[0].reshape(tok_count, head_count, HD)
    local_v = values[0].reshape(tok_count, head_count, HD)
    text_k = text_keys[0].reshape(-1, head_count, HD)
    text_v = text_values[0].reshape(-1, head_count, HD)
    text_count = text_lengths[0]
    query_x, key_x, value_x = (
        lax.all_to_all(local_q, "row", split_axis=1, concat_axis=0, tiled=True),
        lax.all_to_all(local_k, "row", split_axis=1, concat_axis=0, tiled=True),
        lax.all_to_all(local_v, "row", split_axis=1, concat_axis=0, tiled=True),
    )
    head_first = lax.axis_index("row") * query_x.shape[1]
    begin = text_state(query_x, text_k, text_v, text_count, head_first, score_scale)
    folded = key_folder(
        query_x,
        score_scale,
        begin,
        (
            lax.all_gather(key_x, "col", axis=0, tiled=True),
            lax.all_gather(value_x, "col", axis=0, tiled=True),
        ),
    )
    velocity = lax.psum_scatter(
        projector(finish(folded), out_proj, head_first), "row", scatter_dimension=0, tiled=True
    )
    partner = from_partner(velocity, "branch", 0)
    is_cond = lax.axis_index("branch") == 0
    cond_part = jnp.where(is_cond, velocity, partner)
    uncond_part = jnp.where(is_cond, partner, velocity)
    guided_tokens = uncond_part + GUIDE_SCALE * (cond_part - uncond_part)
    frame_count, row_count, col_count, lat_count = latent.shape
    guided = guided_tokens.reshape(frame_count, row_count // 2, col_count // 2, 2, 2, lat_count)
    guided = guided.transpose(0, 1, 3, 2, 4, 5).reshape(
        frame_count, row_count, col_count, lat_count
    )
    index = step_index[0]
    advance = sigma_at(index + 1) - sigma_at(index)
    moved = (latent + advance * guided).astype(jnp.bfloat16)
    rimmed = with_halo(moved, (("row", 1), ("col", 2)), 2)
    padded = jnp.concatenate([rimmed[:1], rimmed[:1], rimmed], 0)
    hidden = conv_taps(padded, conv_in_w, frame_count, row_count + 2, col_count + 2) + conv_in_b
    row_place = lax.axis_index("row") * row_count - 1 + jnp.arange(row_count + 2)
    col_place = lax.axis_index("col") * col_count - 1 + jnp.arange(col_count + 2)
    inside_rows = (row_place >= 0) & (row_place < row_count * lax.axis_size("row"))
    inside_cols = (col_place >= 0) & (col_place < col_count * lax.axis_size("col"))
    inside = inside_rows[:, None] & inside_cols[None, :]
    act = jnp.where(inside[None, :, :, None], jax.nn.silu(hidden), 0.0).astype(jnp.bfloat16)
    act_padded = jnp.concatenate([act[:1], act[:1], act], 0)
    half_count = conv_mid_w.shape[4]
    residual_mid = conv_taps(act_padded, conv_mid_w, frame_count, row_count, col_count)
    own_hidden = lax.dynamic_slice_in_dim(
        hidden[:, 1:-1, 1:-1, :], lax.axis_index("branch") * half_count, half_count, 3
    )
    decoded = own_hidden + residual_mid + conv_mid_b
    return (guided, decoded)


def solution(mesh):
    return jax.shard_map(
        local,
        mesh=mesh,
        in_specs=(
            P("branch", ("row", "col"), None),
            P("branch", ("row", "col"), None),
            P("branch", ("row", "col"), None),
            P("branch", None, None),
            P("branch", None, None),
            P("branch"),
            P(),
            P(),
            P(None, "row", "col", None),
            P(),
            P(),
            P(None, None, None, None, "branch"),
            P("branch"),
        ),
        out_specs=(P(None, "row", "col", None), P(None, "row", "col", "branch")),
        check_vma=False,
    )
```

profile of v0, /device:TPU:1, one launch (start us, length us, event | category | flops | bytes accessed | tf_op | source)
XLA Modules:
  0.0 303.3 jit_solution(11679330131418517302)
XLA Ops:
  7.2 1.1 copy.61
  8.5 23.3 %all_to_all.54 = bf16[96,16,128]{2,0,1:T(8,128)(2,1)} all-to-all(bf16[96,16,128]{2,0,1:T(8,128)(2,1)S(1)} %copy.52), channel_id=1, replica_groups=mesh['branch'=2,'row'=16,'col'=8] {'row'}, dimensions={1} | all-to-all | bytes 786432 | tf_op jit(solution)/shard_map/all_to_all | solution.py:155
  32.0 17.2 %all_to_all.55 = bf16[96,16,128]{2,0,1:T(8,128)(2,1)} all-to-all(bf16[96,16,128]{2,0,1:T(8,128)(2,1)S(1)} %copy.53), channel_id=1, replica_groups=mesh['branch'=2,'row'=16,'col'=8] {'row'}, dimensions={1} | all-to-all | bytes 786432 | tf_op jit(solution)/shard_map/all_to_all | solution.py:156
  50.2 4.2 %all-to-all-start = ((bf16[96,16,128]{2,0,1:T(8,128)(2,1)}), bf16[96,16,128]{2,0,1:T(8,128)(2,1)S(1)}, u32[]{:S(2)}, u32[]{:S(2)}) async-start(bf16[96,16,128]{2,0,1:T(8,128)(2,1)} %copy.49), calls=%async_computation | async-start | bytes 786432 | tf_op jit(solution)/shard_map/all_to_all | solution.py:154
  55.6 1.5 copy.50
  57.1 9.4 %all-to-all-done = bf16[96,16,128]{2,0,1:T(8,128)(2,1)S(1)} async-done(((bf16[96,16,128]{2,0,1:T(8,128)(2,1)}), bf16[96,16,128]{2,0,1:T(8,128)(2,1)S(1)}, u32[]{:S(2)}, u32[]{:S(2)}) %all-to-all-start) | async-done | bytes 393248 | tf_op jit(solution)/shard_map/all_to_all | solution.py:154
  67.7 25.7 %all-gather.5.cloned.1.call-done = bf16[12288,1,128]{2,0,1:T(8,128)(2,1)} async-done(((bf16[1536,1,128]{2,0,1:T(8,128)(2,1)}), bf16[12288,1,128]{2,0,1:T(8,128)(2,1)}) %all-gather.5.cloned.1.call-update) | async-done | bytes 3145744 | tf_op jit(solution)/shard_map/all_gather | solution.py:166
  93.4 66.0 %while.14 = (s32[]{:T(128)}, f32[1536,1]{0,1:T(1,128)S(1)}, f32[1536,1]{0,1:T(1,128)S(1)}, f32[1536,1,128]{0,2,1:T(8,128)S(1)}, bf16[12,1024,1,128]{3,1,2,0:T(8,...) while((s32[]{:T(128)}, f32[1536,1]{0,1:T(1,128)S(1)}, ...), condition=%wide.region_5.6_spmd, body=%wide.region_2.5_spmd.sunk | while | flops 818287104 | bytes 21469284 | solution.py:95
  93.4 1.9 multiply_reduce_fusion.2
  95.4 1.1 fusion.236
  96.5 2.4 fusion.237
  98.9 1.9 multiply_reduce_fusion.2
  100.9 1.1 fusion.236
  102.0 2.4 fusion.237
  104.4 1.9 multiply_reduce_fusion.2
  106.4 1.1 fusion.236
  107.5 2.4 fusion.237
  109.9 1.9 multiply_reduce_fusion.2
  111.9 1.1 fusion.236
  113.0 2.4 fusion.237
  115.4 1.9 multiply_reduce_fusion.2
  118.5 2.4 fusion.237
  120.9 1.9 multiply_reduce_fusion.2
  122.9 1.1 fusion.236
  124.0 2.4 fusion.237
  126.4 1.9 multiply_reduce_fusion.2
  128.4 1.1 fusion.236
  129.5 2.4 fusion.237
  131.9 1.9 multiply_reduce_fusion.2
  133.9 1.1 fusion.236
  135.0 2.4 fusion.237
  137.4 1.9 multiply_reduce_fusion.2
  140.5 2.4 fusion.237
  142.9 1.9 multiply_reduce_fusion.2
  146.0 2.4 fusion.237
  148.4 1.9 multiply_reduce_fusion.2
  151.5 2.4 fusion.237
  153.9 1.9 multiply_reduce_fusion.2
  157.0 2.4 fusion.237
  159.4 1.2 fusion.43
  160.7 60.0 %reduce-scatter.4.cloned.1.call-done = f32[96,64]{1,0:T(8,128)} async-done(((f32[1536,64]{1,0:T(8,128)}), f32[96,64]{1,0:T(8,128)}) %reduce-scatter.4.cloned.1.call-update) | async-done | bytes 24592
  221.5 1.9 collective-permute-start
  224.1 1.9 collective-permute-done
  226.5 1.3 collective-permute-start.2
  227.8 4.0 %collective-permute-start.1 = (bf16[6,2,8,16]{3,2,1,0:T(8,128)(2,1)S(1)}, bf16[6,2,8,16]{3,2,1,0:T(8,128)(2,1)S(1)}, u32[]{:S(2)}, u32[]{:S(2)}) collective-permute-start(bf16[6,2,8,16]{3,2,1,0:T(8,128)(2,1)S(1)} %get-tuple-element.149), channel_id=1, source_target_pairs={{0,8},{8,16},{16,24},{24,32},{32,40},{40,48},{48,56},{56,64},{64,7... | collective-permute-start | bytes 9224 | tf_op jit(solution)/shard_map/ppermute | solution.py:31
  232.8 15.5 %collective-permute-start.4 = (bf16[6,12,2,16]{3,2,1,0:T(2,128)(2,1)S(1)}, bf16[6,12,2,16]{3,2,1,0:T(2,128)(2,1)S(1)}, u32[]{:S(2)}, u32[]{:S(2)}) collective-permute-start(bf16[6,12,2,16]{3,2,1,0:T(2,128)(2,1)S(1)} %get-tuple-element.148), channel_id=1, source_target_pairs={{1,0},{2,1},{3,2},{4,3},{5,4},{6,5},{7,6},{9,8},{10,9},{11,10},{12... | collective-permute-start | bytes 13832 | tf_op jit(solution)/shard_map/ppermute | solution.py:33
  248.3 3.1 %collective-permute-start.3 = (bf16[6,12,2,16]{3,2,1,0:T(2,128)(2,1)S(1)}, bf16[6,12,2,16]{3,2,1,0:T(2,128)(2,1)S(1)}, u32[]{:S(2)}, u32[]{:S(2)}) collective-permute-start(bf16[6,12,2,16]{3,2,1,0:T(2,128)(2,1)S(1)} %get-tuple-element.147), channel_id=1, source_target_pairs={{0,1},{1,2},{2,3},{3,4},{4,5},{5,6},{6,7},{8,9},{9,10},{10,11},{11... | collective-permute-start | bytes 13832 | tf_op jit(solution)/shard_map/ppermute | solution.py:31
  284.1 1.2 pad_maximum_fusion.1
  (227 shorter events, 54.9 us)
Async XLA Ops:
  7.2 152.3 %copy-start = (bf16[2048,64]{0,1:T(8,128)(2,1)S(1)}, bf16[2048,64]{0,1:T(8,128)(2,1)}, u32[]{:S(2)}) copy-start(bf16[2048,64]{0,1:T(8,128)(2,1)} %param.22) | copy-start | bytes 786436
  7.2 60.5 %all-gather.3.cloned.1.call-start = ((), (), s32[]{:S(2)}) async-start(), calls=%async_computation.4 | async-start | bytes 3538944 | tf_op jit(solution)/shard_map/all_gather | solution.py:165
  7.2 24.6 %copy-start.19 = (bf16[1,96,2048]{2,1,0:T(8,128)(2,1)S(1)}, bf16[1,96,2048]{2,1,0:T(8,128)(2,1)}, u32[]{:S(2)}) copy-start(bf16[1,96,2048]{2,1,0:T(8,128)(2,1)} %param.17) | copy-start | bytes 1179652
  31.7 61.7 %all-gather.5.cloned.1.call-start = ((), (), s32[]{:S(2)}) async-start(), calls=%async_computation.5 | async-start | bytes 3538944 | tf_op jit(solution)/shard_map/all_gather | solution.py:166
  31.8 17.4 %copy-start.20 = (bf16[1,96,2048]{2,1,0:T(8,128)(2,1)S(1)}, bf16[1,96,2048]{2,1,0:T(8,128)(2,1)}, u32[]{:S(2)}) copy-start(bf16[1,96,2048]{2,1,0:T(8,128)(2,1)} %param.15) | copy-start | bytes 1179652
  49.2 5.2 %copy-start.2 = (bf16[1,256,2048]{2,1,0:T(8,128)(2,1)S(1)}, bf16[1,256,2048]{2,1,0:T(8,128)(2,1)}, u32[]{:S(2)}) copy-start(bf16[1,256,2048]{2,1,0:T(8,128)(2,1)} %param.18) | copy-start | bytes 3145732
  50.2 16.3 %all-to-all-start = ((bf16[96,16,128]{2,0,1:T(8,128)(2,1)}), bf16[96,16,128]{2,0,1:T(8,128)(2,1)S(1)}, u32[]{:S(2)}, u32[]{:S(2)}) async-start(bf16[96,16,128]{2,0,1:T(8,128)(2,1)} %copy.49), calls=%async_computation | async-start | bytes 786432 | tf_op jit(solution)/shard_map/all_to_all | solution.py:154
  54.4 166.3 %reduce-scatter.4.cloned.1.call-start = ((), (), s32[]{:S(2)}) async-start(), calls=%async_computation.6 | async-start | bytes 835584
  160.6 65.8 %copy-start.21 = (f32[6,8,8,16]{3,2,1,0:T(8,128)S(1)}, f32[6,8,8,16]{3,2,1,0:T(8,128)}, u32[]{:S(2)}) copy-start(f32[6,8,8,16]{3,2,1,0:T(8,128)} %param.23) | copy-start | bytes 73732
  221.5 4.5 %collective-permute-start = (f32[96,64]{0,1:T(8,128)S(1)}, f32[96,64]{0,1:T(8,128)S(1)}, u32[]{:S(2)}, u32[]{:S(2)}) collective-permute-start(f32[96,64]{0,1:T(8,128)S(1)} %copy.59), channel_id=1, source_target_pairs={{0,128},{128,0},{1,129},{129,1},{2,130},{130,2},{3,131},{131,3},{4... | collective-permute-start | bytes 73736 | tf_op jit(solution)/shard_map/ppermute | solution.py:20
  226.4 5.4 %copy-start.3 = (f32[6,4,2,4,2,16]{5,4,3,2,1,0:T(2,128)}, f32[6,4,2,4,2,16]{5,4,3,2,1,0:T(2,128)S(1)}, u32[]{:S(2)}) copy-start(f32[6,4,2,4,2,16]{5,4,3,2,1,0:T(2,128)S(1)} %copy.57) | copy-start | bytes 73732
  226.5 5.3 %collective-permute-start.2 = (bf16[6,2,8,16]{3,2,1,0:T(8,128)(2,1)S(1)}, bf16[6,2,8,16]{3,2,1,0:T(8,128)(2,1)S(1)}, u32[]{:S(2)}, u32[]{:S(2)}) collective-permute-start(bf16[6,2,8,16]{3,2,1,0:T(8,128)(2,1)S(1)} %get-tuple-element.150), channel_id=1, source_target_pairs={{8,0},{16,8},{24,16},{32,24},{40,32},{48,40},{56,48},{64,56},{72,6... | collective-permute-start | bytes 9224 | tf_op jit(solution)/shard_map/ppermute | solution.py:33
  227.8 4.9 %collective-permute-start.1 = (bf16[6,2,8,16]{3,2,1,0:T(8,128)(2,1)S(1)}, bf16[6,2,8,16]{3,2,1,0:T(8,128)(2,1)S(1)}, u32[]{:S(2)}, u32[]{:S(2)}) collective-permute-start(bf16[6,2,8,16]{3,2,1,0:T(8,128)(2,1)S(1)} %get-tuple-element.149), channel_id=1, source_target_pairs={{0,8},{8,16},{16,24},{24,32},{32,40},{40,48},{48,56},{56,64},{64,7... | collective-permute-start | bytes 9224 | tf_op jit(solution)/shard_map/ppermute | solution.py:31
  232.8 18.8 %collective-permute-start.4 = (bf16[6,12,2,16]{3,2,1,0:T(2,128)(2,1)S(1)}, bf16[6,12,2,16]{3,2,1,0:T(2,128)(2,1)S(1)}, u32[]{:S(2)}, u32[]{:S(2)}) collective-permute-start(bf16[6,12,2,16]{3,2,1,0:T(2,128)(2,1)S(1)} %get-tuple-element.148), channel_id=1, source_target_pairs={{1,0},{2,1},{3,2},{4,3},{5,4},{6,5},{7,6},{9,8},{10,9},{11,10},{12... | collective-permute-start | bytes 13832 | tf_op jit(solution)/shard_map/ppermute | solution.py:33
  248.3 4.0 %collective-permute-start.3 = (bf16[6,12,2,16]{3,2,1,0:T(2,128)(2,1)S(1)}, bf16[6,12,2,16]{3,2,1,0:T(2,128)(2,1)S(1)}, u32[]{:S(2)}, u32[]{:S(2)}) collective-permute-start(bf16[6,12,2,16]{3,2,1,0:T(2,128)(2,1)S(1)} %get-tuple-element.147), channel_id=1, source_target_pairs={{0,1},{1,2},{2,3},{3,4},{4,5},{5,6},{6,7},{8,9},{9,10},{10,11},{11... | collective-permute-start | bytes 13832 | tf_op jit(solution)/shard_map/ppermute | solution.py:31
  264.5 1.2 copy-start.5
  265.4 1.3 copy-start.6
  265.4 1.3 copy-start.18
  266.7 0.9 copy-start.4
  269.4 0.9 copy-start.13
  270.3 0.9 copy-start.12
  271.2 0.9 copy-start.11
  272.2 0.9 copy-start.10
  273.1 0.9 copy-start.9
  274.0 0.9 copy-start.8
  274.9 0.9 copy-start.7
  276.4 0.9 copy-start.14
  277.3 0.9 copy-start.17
  278.2 0.9 copy-start.16
  279.1 0.9 copy-start.15
  282.5 0.7 copy-start.22
  285.3 2.2 slice-start
  285.8 2.8 slice-start.1
  295.3 0.7 copy-start.23
  295.6 1.2 copy-start.1
Sparse Core Ops, SparseCore 0:
  31.9 29.2 all-gather.2
  63.0 30.3 all-gather.4
  160.8 59.8 reduce-scatter.3
where the time goes:
time: 306 us; the launch traced here: 303 us
  waiting for transfers between devices  98.7 us (32%)
  matrix products  70.1 us (23%)
  blocking collectives  40.4 us (13%)
  starting transfers between devices  30.2 us (10%)
  local copies, waits for them, and re-layouts  29.4 us (10%)
  other arithmetic  17.9 us (6%)
  between operations  16.2 us (5%)
    unnamed x4, waiting for transfers between devices  60 us
    dot_general x13, matrix products, absorb(): jnp.einsum('qhk,khe->qhe', expo.astype(jnp.bfloat16), value_block, prefer...  29 us
    all_gather x1, waiting for transfers between devices, local(): lax.all_gather(value_x, 'col', axis=0, tiled=True)  25.7 us
    dot_general x13, matrix products, absorb(): jnp.einsum('qhe,khe->qhk', query_block, key_block, preferred_element_type...  23.7 us
    all_to_all x1, blocking collectives, local(): lax.all_to_all(local_k, 'row', split_axis=1, concat_axis=0, tiled=True)  23.3 us
    all_to_all x1, blocking collectives, local(): lax.all_to_all(local_v, 'row', split_axis=1, concat_axis=0, tiled=True)  17.2 us
    ppermute x2, starting transfers between devices, with_halo(): lax.ppermute(head, axis, [((i + 1) % count, i) for i in range(ends)])  16.8 us
    dot_general x54, matrix products, conv_taps(): jnp.dot(window.reshape(-1, window.shape[3]), weight[tap_t, tap_h, tap_w],...  16.3 us
  transfers between devices with their start and end apart: 9, of which 6 were waited for; matrix products, arithmetic and copies ran while one was open for 1% of the time, Pallas kernels for 0%

commit v1 on v0

v1 whole, which is shorter than its diff:
```python
import functools

import jax
import jax.numpy as jnp
import numpy as np
from jax import lax
from jax.experimental import pallas as pl
from jax.experimental.pallas import tpu as pltpu
from jax.sharding import PartitionSpec as P

HD = 128
MESH = pl.DeviceIdType.MESH
NEG_FILL = -1e30
COND_GAIN = 6.0
UNCOND_GAIN = -5.0
SCORE_GAIN = float(HD**-0.5 * np.log2(np.e))

Z_ORDER = (0, 1, 7, 2, 6, 3, 5, 4)
Z_COUNT = 8
SLOTS = 16
TOK = 96
HALF = 48
KV_ROWS = TOK + HALF
GROUPS = 4
PER_GROUP = 4
QUERIES = SLOTS * TOK
CHUNK = 4 * PER_GROUP * TOK
Q_TILE = 512

BF16 = jnp.bfloat16
F32 = jnp.float32


def row_partner(row, slot, sign):
    z, x = row // 2, row % 2
    dz = Z_ORDER[slot // 2]
    dz = dz if sign > 0 else (Z_COUNT - dz) % Z_COUNT
    return lax.rem(z + dz, Z_COUNT) * 2 + lax.rem(x + slot % 2, 2)


def attend(q_ref, o_ref, m_ref, key_ref, value_ref, key_count, usable):
    @pl.loop(0, QUERIES // Q_TILE)
    def _(tile):
        rows = pl.ds(pl.multiple_of(tile * Q_TILE, Q_TILE), Q_TILE)
        scores = lax.dot_general(
            q_ref[rows, :],
            key_ref[0:key_count, :],
            (((1,), (1,)), ((), ())),
            preferred_element_type=F32,
        )
        if usable is not None:
            scores = jnp.where(usable, scores, NEG_FILL)
        before = m_ref[rows, 0:1]
        top = jnp.maximum(before, jnp.max(scores, axis=1, keepdims=True) * SCORE_GAIN)
        weights = jnp.exp2(scores * SCORE_GAIN - top).astype(BF16)
        o_ref[rows, :] = o_ref[rows, :] * jnp.exp2(before - top) + jnp.dot(
            weights, value_ref[0:key_count, :], preferred_element_type=F32
        )
        m_ref[rows, :] = jnp.broadcast_to(top, (Q_TILE, 128))


def attention_kernel(
    q_in, k_in, v_in, w_ref, tk_hbm, tv_hbm, len_ref,
    vel_ref,
    kv_out, q_out, kv, q_ref, o_ref, m_ref, key_ref, value_ref, tk_ref, tv_ref, sh_out, sh_in,
    kv_send, kv_recv, q_send, q_recv, hop_send, hop_recv, sh_send, sh_recv, text_sem,
):
    row, col = lax.axis_index("row"), lax.axis_index("col")
    y, core = col // 2, col % 2
    up = lax.rem(y + 1, 4) * 2 + core
    down = lax.rem(y + 3, 4) * 2 + core
    onward = lax.rem(y + 1 + 2 * core, 4) * 2 + core
    sibling = y * 2 + 1 - core

    barrier = pltpu.get_barrier_semaphore()
    for slot in range(1, SLOTS):
        pl.semaphore_signal(
            barrier, inc=1, device_id={"row": row_partner(row, slot, 1)}, device_id_type=MESH
        )
    for other in (up, down, sibling):
        pl.semaphore_signal(barrier, inc=1, device_id={"col": other}, device_id_type=MESH)

    head_cols = pl.ds(pl.multiple_of(row * HD, HD), HD)
    text_copies = [
        pltpu.make_async_copy(tk_hbm.at[0, :, head_cols], tk_ref, text_sem.at[0]),
        pltpu.make_async_copy(tv_hbm.at[0, :, head_cols], tv_ref, text_sem.at[1]),
    ]
    for copy in text_copies:
        copy.start()

    for head in range(SLOTS):
        cols = slice(head * HD, (head + 1) * HD)
        kv_out[head, 0:TOK, :] = k_in[0, :, cols]
        projected = jnp.dot(v_in[0, :, cols], w_ref[cols, :], preferred_element_type=F32)
        kv_out[head, TOK:KV_ROWS, :] = jnp.concatenate(
            [projected[0:HALF], projected[HALF:TOK]], axis=1
        ).astype(BF16)
        q_out[head] = q_in[0, :, cols]

    def kv_copy(slot):
        there = row_partner(row, slot, 1)
        return pltpu.make_async_remote_copy(
            src_ref=kv_out.at[there],
            dst_ref=kv.at[0, slot],
            send_sem=kv_send.at[slot],
            recv_sem=kv_recv.at[slot],
            device_id={"row": there},
            device_id_type=MESH,
        )

    def q_copy(slot):
        there = row_partner(row, slot, 1)
        return pltpu.make_async_remote_copy(
            src_ref=q_out.at[there],
            dst_ref=q_ref.at[pl.ds(slot * TOK, TOK)],
            send_sem=q_send.at[slot],
            recv_sem=q_recv.at[slot],
            device_id={"row": there},
            device_id_type=MESH,
        )

    def hop_copy(kind, group):
        src, dst, there = (
            (0, 1, up),
            (0, 2, down),
            (1 + core, 3, onward),
            (0, 4, sibling),
            (1, 5, sibling),
            (2, 6, sibling),
            (3, 7, sibling),
        )[kind]
        part = pl.ds(group * PER_GROUP, PER_GROUP)
        return pltpu.make_async_remote_copy(
            src_ref=kv.at[src, part],
            dst_ref=kv.at[dst, part],
            send_sem=hop_send.at[kind, group],
            recv_sem=hop_recv.at[kind, group],
            device_id={"col": there},
            device_id_type=MESH,
        )

    def share_copy(slot):
        return pltpu.make_async_remote_copy(
            src_ref=sh_out.at[slot],
            dst_ref=sh_in.at[slot],
            send_sem=sh_send.at[slot],
            recv_sem=sh_recv.at[slot],
            device_id={"row": row_partner(row, slot, -1)},
            device_id_type=MESH,
        )

    pl.semaphore_wait(barrier, SLOTS - 1 + 3)
    for slot in range(1, PER_GROUP):
        kv_copy(slot).start()
    for slot in range(1, SLOTS):
        q_copy(slot).start()
    for slot in range(PER_GROUP, SLOTS):
        kv_copy(slot).start()

    kv[0, 0] = kv_out[row]
    q_ref[0:TOK, :] = q_out[row]
    o_ref[...] = jnp.zeros_like(o_ref)
    m_ref[...] = jnp.full_like(m_ref, NEG_FILL)

    lane = lax.broadcasted_iota(jnp.int32, (HALF, HD), 1)
    ones = jnp.where(lane == HD // 2, 1.0, 0.0).astype(F32)

    def first_hop(group):
        for slot in range(group * PER_GROUP, (group + 1) * PER_GROUP):
            if slot:
                kv_copy(slot).wait_recv()
        for kind in (0, 1, 3):
            hop_copy(kind, group).start()

    def second_hop(group):
        hop_copy(0, group).wait_recv()
        hop_copy(1, group).wait_recv()
        for kind in (2, 4, 5):
            hop_copy(kind, group).start()

    def third_hop(group):
        hop_copy(2, group).wait_recv()
        hop_copy(6, group).start()

    def from_sibling(group):
        for kind in (3, 4, 5, 6):
            hop_copy(kind, group).wait_recv()

    first_hop(0)

    for copy in text_copies:
        copy.wait()
    text_rows = tk_ref.shape[0]
    own_proj = w_ref[pl.ds(pl.multiple_of(row * HD, HD), HD), :]
    text_projected = jnp.dot(tv_ref[...], own_proj, preferred_element_type=F32)
    text_lane = lax.broadcasted_iota(jnp.int32, (text_rows, HD // 2), 1)
    value_ref[0:text_rows, :] = jnp.concatenate(
        [text_projected, jnp.where(text_lane == 0, 1.0, 0.0).astype(F32)], axis=1
    ).astype(BF16)
    for slot in range(1, SLOTS):
        q_copy(slot).wait_recv()
    usable = lax.broadcasted_iota(jnp.int32, (Q_TILE, text_rows), 1) < len_ref[0]
    attend(q_ref, o_ref, m_ref, tk_ref, value_ref, text_rows, usable)

    second_hop(0)
    first_hop(1)
    third_hop(0)

    def before_chunk_1():
        second_hop(1)
        first_hop(2)
        from_sibling(0)

    def before_chunk_2():
        third_hop(1)
        second_hop(2)
        first_hop(3)

    def before_chunk_3():
        third_hop(2)
        second_hop(3)
        from_sibling(1)

    def before_chunk_4():
        third_hop(3)

    def before_chunk_5():
        from_sibling(2)

    def before_chunk_7():
        from_sibling(3)

    steps = {
        1: before_chunk_1,
        2: before_chunk_2,
        3: before_chunk_3,
        4: before_chunk_4,
        5: before_chunk_5,
        7: before_chunk_7,
    }

    @pl.loop(0, 2 * GROUPS)
    def _(chunk):
        for when, step in steps.items():
            pl.when(chunk == when)(step)
        group, side = chunk // 2, chunk % 2

        for part in range(4):
            for slot in range(PER_GROUP):
                at = (part * PER_GROUP + slot) * TOK
                block = kv.at[4 * side + part, group * PER_GROUP + slot]
                key_ref[at : at + TOK, :] = block[0:TOK, :]
                packed = block[TOK:KV_ROWS, :].astype(F32)
                value_ref[at : at + HALF, :] = jnp.where(lane < HD // 2, packed, ones).astype(BF16)
                value_ref[at + HALF : at + TOK, :] = jnp.where(
                    lane < HD // 2, pltpu.roll(packed, HD // 2, 1), ones
                ).astype(BF16)
        attend(q_ref, o_ref, m_ref, key_ref, value_ref, CHUNK, None)

    total = None
    for slot in range(SLOTS):
        out = o_ref[slot * TOK : (slot + 1) * TOK, :]
        share = out[:, 0 : HD // 2] / out[:, HD // 2 : HD // 2 + 1]
        packed = jnp.concatenate([share[0:HALF], share[HALF:TOK]], axis=1)
        if slot == 0:
            total = packed
        else:
            sh_out[slot] = packed.astype(BF16)
            share_copy(slot).start()
    for slot in range(1, SLOTS):
        share_copy(slot).wait_recv()
        total = total + sh_in[slot].astype(F32)
    vel_ref[...] = total

    for slot in range(1, SLOTS):
        kv_copy(slot).wait_send()
        q_copy(slot).wait_send()
        share_copy(slot).wait_send()
    for group in range(GROUPS):
        for kind in range(7):
            hop_copy(kind, group).wait_send()


def tile_velocity(queries, keys, values, out_proj, text_keys, text_values, text_lengths):
    text_rows = text_keys.shape[1]
    vmem = pl.BlockSpec(memory_space=pltpu.VMEM)
    dma = pltpu.SemaphoreType.DMA
    return pl.pallas_call(
        attention_kernel,
        out_shape=jax.ShapeDtypeStruct((HALF, HD), F32),
        in_specs=[
            vmem, vmem, vmem, vmem,
            pl.BlockSpec(memory_space=pl.ANY),
            pl.BlockSpec(memory_space=pl.ANY),
            pl.BlockSpec(memory_space=pltpu.SMEM),
        ],
        out_specs=vmem,
        scratch_shapes=[
            pltpu.VMEM((SLOTS, KV_ROWS, HD), BF16),
            pltpu.VMEM((SLOTS, TOK, HD), BF16),
            pltpu.VMEM((8, SLOTS, KV_ROWS, HD), BF16),
            pltpu.VMEM((QUERIES, HD), BF16),
            pltpu.VMEM((QUERIES, HD), F32),
            pltpu.VMEM((QUERIES, HD), F32),
            pltpu.VMEM((CHUNK, HD), BF16),
            pltpu.VMEM((CHUNK, HD), BF16),
            pltpu.VMEM((text_rows, HD), BF16),
            pltpu.VMEM((text_rows, HD), BF16),
            pltpu.VMEM((SLOTS, HALF, HD), BF16),
            pltpu.VMEM((SLOTS, HALF, HD), BF16),
            dma((SLOTS,)), dma((SLOTS,)), dma((SLOTS,)), dma((SLOTS,)),
            dma((7, GROUPS)), dma((7, GROUPS)), dma((SLOTS,)), dma((SLOTS,)), dma((2,)),
        ],
        compiler_params=pltpu.CompilerParams(
            collective_id=0, has_side_effects=True, vmem_limit_bytes=50 * 2**20
        ),
        name="attention",
    )(queries, keys, values, out_proj, text_keys, text_values, text_lengths)


AROUND = tuple((dr, dc) for dr in (-1, 0, 1) for dc in (-1, 0, 1))
FRAMES, TROWS, TCOLS = 6, 4, 4
PLACES = TROWS * TCOLS
ROWS = FRAMES * PLACES
PADDED_ROWS = (FRAMES + 2) * PLACES


def pick_matrix():
    pick = np.zeros((3, 3, FRAMES // 2, TROWS, TCOLS, 9, FRAMES // 2, TROWS, TCOLS), np.float32)
    for e, g, f, i, j in np.ndindex(3, 3, FRAMES // 2, TROWS, TCOLS):
        r, c = i + e - 1, j + g - 1
        tile = AROUND.index((r // TROWS, c // TCOLS))
        pick[e, g, f, i, j, tile, f, r % TROWS, c % TCOLS] = 1.0
    return pick.reshape(9 * HALF, 9 * HALF)


def sigma_at(index):
    s = 1.0 - index / 50.0
    return 7.0 * s / (1.0 + 6.0 * s)


def decoder_kernel(
    row_count, col_count,
    vel_ref, lat_ref, pick_ref, step_ref, win_ref, bin_ref, wmid_hbm, bmid_ref,
    guided_ref, out_ref,
    mine, raw, raw_in, near, moved, shifted, w_in, wmid, act, center,
    send, recv, w_sem,
):
    branch, row, col = lax.axis_index("branch"), lax.axis_index("row"), lax.axis_index("col")

    def place(side, tile):
        dr, dc = AROUND[tile]
        return {
            "branch": lax.rem(branch + side, 2),
            "row": lax.rem(row + dr + row_count, row_count),
            "col": lax.rem(col + dc + col_count, col_count),
        }

    peers = [(side, tile) for side in (0, 1) for tile in range(9) if (side, tile) != (0, 4)]

    barrier = pltpu.get_barrier_semaphore()
    for side, tile in peers:
        pl.semaphore_signal(barrier, inc=1, device_id=place(side, tile), device_id_type=MESH)

    w_copies = []
    for b in range(3):
        for c in range(3):
            for a in range(3):
                at = (b * 3 + c) * 3 + a
                w_copies.append(
                    pltpu.make_async_copy(
                        wmid_hbm.at[a, b, c],
                        wmid.at[b * 3 + c, pl.ds(a * 512, 512)],
                        w_sem.at[at],
                    )
                )
    for copy in w_copies:
        copy.start()

    index = step_ref[0].astype(F32)
    advance = sigma_at(index + 1.0) - sigma_at(index)
    first = branch == 0
    velocity = vel_ref[...]
    raw[...] = velocity
    keep = jnp.where(first, 1.0, 0.0)
    gain = jnp.where(first, COND_GAIN, UNCOND_GAIN) * advance
    mine[...] = lat_ref[...] * keep + velocity * gain

    def copy_to(side, tile):
        if tile == 4:
            src, dst = raw, raw_in
        else:
            src, dst = mine, near.at[side, 8 - tile]
        return pltpu.make_async_remote_copy(
            src_ref=src,
            dst_ref=dst,
            send_sem=send.at[side, tile],
            recv_sem=recv.at[side, tile],
            device_id=place(side, tile),
            device_id_type=MESH,
        )

    pl.semaphore_wait(barrier, len(peers))
    for side, tile in peers:
        copy_to(side, tile).start()

    zero = jnp.zeros((16, 512), BF16)
    for a in range(3):
        for r in range(4):
            for c in range(4):
                lanes = (((r // 2) * 2 + c // 2) * 4 + (r % 2) * 2 + c % 2) * 16
                for pp in range(2):
                    for ss in range(2):
                        inside = 0 <= r - pp < 3 and 0 <= c - ss < 3
                        w_in[
                            a * 256 + lanes : a * 256 + lanes + 16,
                            (pp * 2 + ss) * 512 : (pp * 2 + ss + 1) * 512,
                        ] = win_ref[a, r - pp, c - ss] if inside else zero

    for side, tile in peers:
        copy_to(side, tile).wait_recv()

    cond = jnp.where(first, raw[...], raw_in[...])
    uncond = jnp.where(first, raw_in[...], raw[...])
    guided = COND_GAIN * cond + UNCOND_GAIN * uncond
    guided_ref[...] = guided
    for tile, (dr, dc) in enumerate(AROUND):
        if tile == 4:
            value = lat_ref[...] + advance * guided
        else:
            there_row, there_col = row + dr, col + dc
            there = (
                (there_row >= 0)
                & (there_row < row_count)
                & (there_col >= 0)
                & (there_col < col_count)
            )
            value = (near[0, tile] + near[1, tile]) * jnp.where(there, 1.0, 0.0)
        moved[tile * HALF : (tile + 1) * HALF, :] = value.astype(BF16)

    picked = jnp.dot(pick_ref[...], moved[...], preferred_element_type=F32)
    lane = lax.broadcasted_iota(jnp.int32, (HALF, HD), 1)
    low = lane < HD // 2
    for e in range(3):
        for g in range(2):
            at = (e * 3 + g) * HALF
            here, right = picked[at : at + HALF], picked[at + HALF : at + 2 * HALF]
            early = jnp.where(low, here, pltpu.roll(right, HD // 2, 1)).astype(BF16)
            late = jnp.where(low, pltpu.roll(here, HD // 2, 1), right).astype(BF16)
            shifted[e, g, 0:PLACES, :] = early[0:PLACES]
            shifted[e, g, PLACES : 2 * PLACES, :] = early[0:PLACES]
            shifted[e, g, 2 * PLACES : 2 * PLACES + HALF, :] = early
            shifted[e, g, 2 * PLACES + HALF : PADDED_ROWS, :] = late

    patches = jnp.concatenate(
        [
            jnp.concatenate(
                [
                    shifted[db + du, dc, a * PLACES : a * PLACES + ROWS, :]
                    for a in range(3)
                    for du in range(2)
                ],
                axis=1,
            )
            for db in range(2)
            for dc in range(2)
        ],
        axis=0,
    )

    at = lax.broadcasted_iota(jnp.int32, (ROWS, 1), 0)
    row_at, col_at = (at // TCOLS) % TROWS, at % TCOLS
    bias_in = bin_ref[...]
    for pp in range(2):
        for ss in range(2):
            kind = pp * 2 + ss
            for half in range(2):
                cols = slice(half * 256, (half + 1) * 256)
                hidden = (
                    jnp.dot(
                        patches,
                        w_in[:, kind * 512 + half * 256 : kind * 512 + (half + 1) * 256],
                        preferred_element_type=F32,
                    )
                    + bias_in[:, cols]
                )
                for db in range(2):
                    for dc in range(2):
                        shift = db * 2 + dc
                        block = hidden[shift * ROWS : (shift + 1) * ROWS]
                        if (db, dc) == (1 - pp, 1 - ss):
                            center[kind, :, cols] = block
                        y_at = row * (2 * TROWS) - 1 + 2 * (row_at + db) + pp
                        x_at = col * (2 * TCOLS) - 1 + 2 * (col_at + dc) + ss
                        inside = (
                            (y_at >= 0)
                            & (y_at < row_count * 2 * TROWS)
                            & (x_at >= 0)
                            & (x_at < col_count * 2 * TCOLS)
                        )
                        value = jnp.where(inside, block * jax.nn.sigmoid(block), 0.0).astype(BF16)
                        act[kind, shift, 0:PLACES, cols] = value[0:PLACES]
                        act[kind, shift, PLACES : 2 * PLACES, cols] = value[0:PLACES]
                        act[kind, shift, 2 * PLACES : PADDED_ROWS, cols] = value

    total = None
    for b in range(3):
        for c in range(3):
            for a in range(3):
                w_copies[(b * 3 + c) * 3 + a].wait()
            window = []
            for pi in range(2):
                for si in range(2):
                    kind = ((pi + b) % 2) * 2 + (si + c) % 2
                    shift = ((pi + b) // 2) * 2 + (si + c) // 2
                    window.append(
                        jnp.concatenate(
                            [
                                act[kind, shift, a * PLACES : a * PLACES + ROWS, :]
                                for a in range(3)
                            ],
                            axis=1,
                        )
                    )
            term = jnp.dot(
                jnp.concatenate(window, axis=0), wmid[b * 3 + c], preferred_element_type=F32
            )
            total = term if total is None else total + term
    own = pl.ds(pl.multiple_of(branch * 256, 256), 256)
    for pi in range(2):
        for si in range(2):
            phase = pi * 2 + si
            out_ref[phase] = (
                center[(1 - pi) * 2 + (1 - si), :, own]
                + total[phase * ROWS : (phase + 1) * ROWS]
                + bmid_ref[...]
            )

    for side, tile in peers:
        copy_to(side, tile).wait_send()


def decode(velocity, latent_tile, step_index, w_in, b_in, w_mid, b_mid, row_count, col_count):
    vmem = pl.BlockSpec(memory_space=pltpu.VMEM)
    dma = pltpu.SemaphoreType.DMA
    return pl.pallas_call(
        functools.partial(decoder_kernel, row_count, col_count),
        out_shape=(
            jax.ShapeDtypeStruct((HALF, HD), F32),
            jax.ShapeDtypeStruct((4, ROWS, 256), F32),
        ),
        in_specs=[
            vmem, vmem, vmem,
            pl.BlockSpec(memory_space=pltpu.SMEM),
            vmem, vmem,
            pl.BlockSpec(memory_space=pl.ANY),
            vmem,
        ],
        out_specs=(vmem, vmem),
        scratch_shapes=[
            pltpu.VMEM((HALF, HD), F32),
            pltpu.VMEM((HALF, HD), F32),
            pltpu.VMEM((HALF, HD), F32),
            pltpu.VMEM((2, 9, HALF, HD), F32),
            pltpu.VMEM((9 * HALF, HD), BF16),
            pltpu.VMEM((3, 2, PADDED_ROWS, HD), BF16),
            pltpu.VMEM((768, 2048), BF16),
            pltpu.VMEM((9, 1536, 256), BF16),
            pltpu.VMEM((4, 4, PADDED_ROWS, 512), BF16),
            pltpu.VMEM((4, ROWS, 512), F32),
            dma((2, 9)), dma((2, 9)), dma((27,)),
        ],
        compiler_params=pltpu.CompilerParams(
            collective_id=1, has_side_effects=True, vmem_limit_bytes=50 * 2**20
        ),
        name="decoder",
    )(
        velocity, latent_tile, jnp.asarray(pick_matrix(), BF16), step_index,
        w_in, b_in[None, :], w_mid, b_mid[None, :],
    )


def local(
    row_count,
    col_count,
    queries,
    keys,
    values,
    text_keys,
    text_values,
    text_lengths,
    step_index,
    out_proj,
    latent,
    conv_in_w,
    conv_in_b,
    conv_mid_w,
    conv_mid_b,
):
    latent_tile = (
        latent.reshape(2, 3, TROWS, 2, TCOLS, 2, 16)
        .transpose(1, 2, 4, 0, 3, 5, 6)
        .reshape(HALF, HD)
    )
    velocity = tile_velocity(queries, keys, values, out_proj, text_keys, text_values, text_lengths)
    guided, decoded = decode(
        velocity, latent_tile, step_index, conv_in_w, conv_in_b, conv_mid_w, conv_mid_b,
        row_count, col_count,
    )
    guided = (
        guided.reshape(3, TROWS, TCOLS, 2, 2, 2, 16)
        .transpose(3, 0, 1, 4, 2, 5, 6)
        .reshape(latent.shape)
    )
    decoded = (
        decoded.reshape(2, 2, FRAMES, TROWS, TCOLS, 256)
        .transpose(2, 3, 0, 4, 1, 5)
        .reshape(FRAMES, 2 * TROWS, 2 * TCOLS, 256)
    )
    return guided, decoded


def solution(mesh):
    return jax.shard_map(
        functools.partial(local, mesh.shape["row"], mesh.shape["col"]),
        mesh=mesh,
        in_specs=(
            P("branch", ("row", "col"), None),
            P("branch", ("row", "col"), None),
            P("branch", ("row", "col"), None),
            P("branch", None, None),
            P("branch", None, None),
            P("branch"),
            P(),
            P(),
            P(None, "row", "col", None),
            P(),
            P(),
            P(None, None, None, None, "branch"),
            P("branch"),
        ),
        out_specs=(P(None, "row", "col", None), P(None, "row", "col", "branch")),
        check_vma=False,
    )
```

time: 306 us -> 120 us (0.39)
  Pallas kernels: 0 us -> 103 us
  waiting for transfers between devices: 98.7 us -> 0 us
  matrix products: 70.1 us -> 0 us
  blocking collectives: 40.4 us -> 0 us
  starting transfers between devices: 30.2 us -> 0 us
  other arithmetic: 17.9 us -> 0 us
  local copies, waits for them, and re-layouts: 29.4 us -> 13.8 us
  between operations: 16.2 us -> 2.02 us
    pallas_call x0 -> x2, Pallas kernels: none -> 103 us  [the longest x1 76.5 us: tile_velocity(): pl.pallas_call(attention_kernel, out_shape=jax.ShapeDtypeStruct((HALF, HD...]
    dot_general x80 -> x0, matrix products: 68.9 us -> none  [the longest x13 29 us: absorb(): jnp.einsum('qhk,khe->qhe', expo.astype(jnp.bfloat16), value_block, prefer...]
    unnamed x4 -> x0, waiting for transfers between devices: 60 us -> none
    all_to_all x2 -> x0, blocking collectives: 40.4 us -> none  [the longest x1 23.3 us: local(): lax.all_to_all(local_k, 'row', split_axis=1, concat_axis=0, tiled=True)]
    ppermute x5 -> x0, starting transfers between devices: 25.8 us -> none  [the longest x2 16.8 us: with_halo(): lax.ppermute(head, axis, [((i + 1) % count, i) for i in range(ends)])]
    all_gather x2 -> x0, waiting for transfers between devices: 25.7 us -> none  [the longest x1 25.7 us: local(): lax.all_gather(value_x, 'col', axis=0, tiled=True)]
    reduce_sum x13 -> x0, other arithmetic: 13.2 us -> none  [absorb(): running_sum = running_sum * factor + jnp.sum(expo, axis=2)]
    all_to_all x1 -> x0, waiting for transfers between devices: 9.36 us -> none  [local(): lax.all_to_all(local_q, 'row', split_axis=1, concat_axis=0, tiled=True)]
  transfers between devices with their start and end apart: 9 -> 0, of which waited for: 6 -> 0; matrix products, arithmetic and copies ran while one was open for 1% -> 0% of each run, Pallas kernels for 0% -> 0%
where the time goes in v1:
time: 120 us; the launch traced here: 119 us
  Pallas kernels  103 us (86%)
  local copies, waits for them, and re-layouts  13.8 us (12%)
  between operations  2.02 us (2%)
    pallas_call x1, Pallas kernels, tile_velocity(): pl.pallas_call(attention_kernel, out_shape=jax.ShapeDtypeStruct((HALF, HD...  76.5 us
    pallas_call x1, Pallas kernels, decode(): pl.pallas_call(functools.partial(decoder_kernel, row_count, col_count), o...  26.9 us
    unnamed x19, local copies, waits for them, and re-layouts  10 us

profile of v1, /device:TPU:1, one launch (start us, length us, event | category | flops | bytes accessed | tf_op | source)
XLA Modules:
  0.0 119.2 jit_solution(16936636334776445772)
XLA Ops:
  0.6 1.2 %copy.16.w_ref = bf16[2048,64]{1,0:T(8,128)(2,1)S(1)} copy(bf16[2048,64]{0,1:T(8,128)(2,1)} %param.21) | data formatting | bytes 524288 | tf_op args[7]
  2.5 0.0 copy-start
  2.5 1.2 %copy-done = bf16[1,256,2048]{2,1,0:T(8,128)(2,1)S(1)} copy-done((bf16[1,256,2048]{2,1,0:T(8,128)(2,1)S(1)}, bf16[1,256,2048]{2,1,0:T(8,128)(2,1)}, u32[]{:S(2)}) %copy-start) | copy-done | bytes 1048600
  3.7 0.0 copy-start.1
  3.7 1.2 %copy-done.1 = bf16[1,256,2048]{2,1,0:T(8,128)(2,1)S(1)} copy-done((bf16[1,256,2048]{2,1,0:T(8,128)(2,1)S(1)}, bf16[1,256,2048]{2,1,0:T(8,128)(2,1)}, u32[]{:S(2)}) %copy-start.1) | copy-done | bytes 1048600
  5.0 0.0 copy-start.4
  5.0 1.0 copy-done.4
  6.0 0.0 copy-start.5
  6.0 1.0 copy-done.5
  7.0 0.0 copy-start.6
  7.0 1.0 copy-done.6
  8.0 76.5 %attention.1.vel_ref = f32[48,128]{1,0:T(8,128)S(1)} custom-call(bf16[1,96,2048]{2,1,0:T(8,128)(2,1)S(1)} %copy-done.4, bf16[1,96,2048]{2,1,0:T(8,128)(2,1)S(1)} %copy-done.5, bf16[1,96,2048]{2,1,0:T(8,128)(2,1)S(1)} %copy-done.6, bf16[2048,64]{1,0:T(8,128)(2,1)S(1)} %copy.16.w_ref, bf16[1,256,2048]{2,1,0:T(8,128)(2,1)S(1)} %copy-done, ...), custom_call_target="tpu_custom_call" | custom-call | tf_op jit(solution)/shard_map/attention/pallas_call | solution.py:288
  84.4 1.0 copy.21
  85.5 0.2 reshape.23.lat_ref
  86.3 0.0 copy-start.2
  86.4 1.0 copy-done.2
  87.4 0.0 copy-start.3
  87.4 1.0 copy-done.3
  88.4 0.0 copy-start.7
  88.4 0.7 copy-done.7
  89.1 0.0 copy-start.8
  89.1 0.7 copy-done.8
  89.7 26.9 %decoder.1 = (f32[48,128]{1,0:T(8,128)S(1)}, f32[4,96,256]{2,1,0:T(8,128)S(1)}) custom-call(f32[48,128]{1,0:T(8,128)S(1)} %attention.1.vel_ref, f32[48,128]{1,0:T(8,128)S(1)} %reshape.23.lat_ref, bf16[432,432]{1,0:T(8,128)(2,1)S(1)} %copy-done.3, s32[1]{0:T(128)S(6)} %copy.23.step_ref, bf16[3,3,3,16,512]{4,3,2,1,0:T(8,128)(2,1)S(1)} %copy-done.2, ...), custom_call_target="tpu_custom_call" | custom-call | tf_op jit(solution)/shard_map/decoder/pallas_call | solution.py:546
  116.7 0.1 reshape.26
  116.8 0.3 copy.19
  117.1 1.0 reshape.27
  118.1 0.3 reshape.24
  118.4 0.7 copy.18
Async XLA Ops:
  2.5 1.2 %copy-start = (bf16[1,256,2048]{2,1,0:T(8,128)(2,1)S(1)}, bf16[1,256,2048]{2,1,0:T(8,128)(2,1)}, u32[]{:S(2)}) copy-start(bf16[1,256,2048]{2,1,0:T(8,128)(2,1)} %tk_hbm.1) | copy-start | bytes 3145732
  3.7 1.2 %copy-start.1 = (bf16[1,256,2048]{2,1,0:T(8,128)(2,1)S(1)}, bf16[1,256,2048]{2,1,0:T(8,128)(2,1)}, u32[]{:S(2)}) copy-start(bf16[1,256,2048]{2,1,0:T(8,128)(2,1)} %tv_hbm.1) | copy-start | bytes 3145732
  5.0 1.0 copy-start.4
  6.0 1.0 copy-start.5
  7.0 1.0 copy-start.6
  86.3 1.0 copy-start.2
  87.4 1.0 copy-start.3
  88.4 0.7 copy-start.7
  89.1 0.7 copy-start.8

commit v2 on v1

v2 whole, which is shorter than its diff:
```python
import functools

import jax
import jax.numpy as jnp
import numpy as np
from jax import lax
from jax.experimental import pallas as pl
from jax.experimental.pallas import tpu as pltpu
from jax.sharding import PartitionSpec as P

HD = 128
MESH = pl.DeviceIdType.MESH
NEG_FILL = -1e30
COND_GAIN = 6.0
UNCOND_GAIN = -5.0
SCORE_GAIN = float(HD**-0.5 * np.log2(np.e))

Z_ORDER = (0, 1, 7, 2, 6, 3, 5, 4)
Z_COUNT = 8
SLOTS = 16
TOK = 96
HALF = 48
KV_ROWS = TOK + HALF
GROUPS = 4
PER_GROUP = 4
QUERIES = SLOTS * TOK
CHUNK = 4 * PER_GROUP * TOK
PART = QUERIES // 2

BF16 = jnp.bfloat16
F32 = jnp.float32


def row_partner(row, slot, sign):
    z, x = row // 2, row % 2
    dz = Z_ORDER[slot // 2]
    dz = dz if sign > 0 else (Z_COUNT - dz) % Z_COUNT
    return lax.rem(z + dz, Z_COUNT) * 2 + lax.rem(x + slot % 2, 2)


AROUND = tuple((dr, dc) for dr in (-1, 0, 1) for dc in (-1, 0, 1))
FRAMES, TROWS, TCOLS = 6, 4, 4
PLACES = TROWS * TCOLS
ROWS = FRAMES * PLACES
PADDED_ROWS = (FRAMES + 2) * PLACES


def pick_matrix():
    pick = np.zeros((3, 3, FRAMES // 2, TROWS, TCOLS, 9, FRAMES // 2, TROWS, TCOLS), np.float32)
    for e, g, f, i, j in np.ndindex(3, 3, FRAMES // 2, TROWS, TCOLS):
        r, c = i + e - 1, j + g - 1
        tile = AROUND.index((r // TROWS, c // TCOLS))
        pick[e, g, f, i, j, tile, f, r % TROWS, c % TCOLS] = 1.0
    return pick.reshape(9 * HALF, 9 * HALF)


def sigma_at(index):
    s = 1.0 - index / 50.0
    return 7.0 * s / (1.0 + 6.0 * s)


def attend(q_ref, o_ref, m_ref, part, key_ref, value_ref, usable):
    rows = pl.ds(pl.multiple_of(part * PART, PART), PART)
    scores = lax.dot_general(
        q_ref[rows, :], key_ref[...], (((1,), (1,)), ((), ())), preferred_element_type=F32
    )
    if usable is not None:
        scores = jnp.where(usable, scores, NEG_FILL)
    before = m_ref[rows, :]
    top = jnp.maximum(before, jnp.max(scores, axis=1, keepdims=True) * SCORE_GAIN)
    wide = jnp.concatenate([top] * (scores.shape[1] // HD), axis=1)
    weights = jnp.exp2(scores * SCORE_GAIN - wide).astype(BF16)
    o_ref[rows, :] = o_ref[rows, :] * jnp.exp2(before - top) + jnp.dot(
        weights, value_ref[...], preferred_element_type=F32
    )
    m_ref[rows, :] = top


def step_kernel(
    row_count, col_count,
    q_hbm, k_hbm, v_hbm, w_hbm, tk_hbm, tv_hbm, len_ref,
    lat_hbm, pick_hbm, step_ref, win_hbm, bin_hbm, wmid_hbm, bmid_hbm,
    guided_ref, out_ref,
    v_ref, w_ref, v_out, kv, q_ref, o_ref, m_ref, key_ref, value_ref, tk_ref, tv_ref, text_value, sh_out, sh_in,
    lat_in, pieces, lat_ref, pick_ref, win_ref, bin_ref, bmid_ref,
    mine, raw, raw_in, around, moved, shifted, w_in, wmid, act, center, ordered,
    k_send, k_recv, v_send, v_recv, q_send, q_recv, hop_send, hop_recv, sh_send, sh_recv,
    send, recv, w_sem, in_sem,
):
    branch, row, col = lax.axis_index("branch"), lax.axis_index("row"), lax.axis_index("col")
    y, core = col // 2, col % 2
    up = lax.rem(y + 1, 4) * 2 + core
    down = lax.rem(y + 3, 4) * 2 + core
    opposite = lax.rem(y + 2, 4) * 2 + core
    sibling = y * 2 + 1 - core

    def place(side, tile):
        dr, dc = AROUND[tile]
        return {
            "branch": lax.rem(branch + side, 2),
            "row": lax.rem(row + dr + row_count, row_count),
            "col": lax.rem(col + dc + col_count, col_count),
        }

    peers = [(side, tile) for side in (0, 1) for tile in range(9) if (side, tile) != (0, 4)]

    barrier = pltpu.get_barrier_semaphore()
    for slot in range(1, SLOTS):
        pl.semaphore_signal(
            barrier, inc=1, device_id={"row": row_partner(row, slot, 1)}, device_id_type=MESH
        )
    for other in (up, down, opposite, sibling):
        pl.semaphore_signal(barrier, inc=1, device_id={"col": other}, device_id_type=MESH)
    for side, tile in peers:
        pl.semaphore_signal(barrier, inc=1, device_id=place(side, tile), device_id_type=MESH)

    head_cols = pl.ds(pl.multiple_of(row * HD, HD), HD)
    loads = [
        pltpu.make_async_copy(src, dst, in_sem.at[i])
        for i, (src, dst) in enumerate(
            (
                (v_hbm.at[0], v_ref),
                (w_hbm, w_ref),
                (k_hbm.at[0, :, head_cols], kv.at[0, 0, pl.ds(0, TOK)]),
                (q_hbm.at[0, :, head_cols], q_ref.at[pl.ds(0, TOK)]),
                (tk_hbm.at[0, :, head_cols], tk_ref),
                (tv_hbm.at[0, :, head_cols], tv_ref),
                (win_hbm, win_ref),
                (bin_hbm, bin_ref),
                (bmid_hbm, bmid_ref),
                (pick_hbm, pick_ref),
                (lat_hbm, lat_in),
            )
        )
    ]
    for copy in loads:
        copy.start()

    def k_copy(slot):
        there = row_partner(row, slot, 1)
        return pltpu.make_async_remote_copy(
            src_ref=k_hbm.at[0, :, pl.ds(pl.multiple_of(there * HD, HD), HD)],
            dst_ref=kv.at[0, slot, pl.ds(0, TOK)],
            send_sem=k_send.at[slot],
            recv_sem=k_recv.at[slot],
            device_id={"row": there},
            device_id_type=MESH,
        )

    def v_copy(slot):
        there = row_partner(row, slot, 1)
        return pltpu.make_async_remote_copy(
            src_ref=v_out.at[there],
            dst_ref=kv.at[0, slot, pl.ds(TOK, HALF)],
            send_sem=v_send.at[slot],
            recv_sem=v_recv.at[slot],
            device_id={"row": there},
            device_id_type=MESH,
        )

    def q_copy(slot):
        there = row_partner(row, slot, 1)
        return pltpu.make_async_remote_copy(
            src_ref=q_hbm.at[0, :, pl.ds(pl.multiple_of(there * HD, HD), HD)],
            dst_ref=q_ref.at[pl.ds(slot * TOK, TOK)],
            send_sem=q_send.at[slot],
            recv_sem=q_recv.at[slot],
            device_id={"row": there},
            device_id_type=MESH,
        )

    def hop_copy(kind, group):
        src, dst, there = (
            (0, 1, up),
            (0, 2, down),
            (0, 3, opposite),
            (0, 4, sibling),
            (1, 5, sibling),
            (2, 6, sibling),
            (3, 7, sibling),
        )[kind]
        part = pl.ds(group * PER_GROUP, PER_GROUP)
        return pltpu.make_async_remote_copy(
            src_ref=kv.at[src, part],
            dst_ref=kv.at[dst, part],
            send_sem=hop_send.at[kind, group],
            recv_sem=hop_recv.at[kind, group],
            device_id={"col": there},
            device_id_type=MESH,
        )

    def share_copy(slot):
        return pltpu.make_async_remote_copy(
            src_ref=sh_out.at[slot],
            dst_ref=sh_in.at[slot],
            send_sem=sh_send.at[slot],
            recv_sem=sh_recv.at[slot],
            device_id={"row": row_partner(row, slot, -1)},
            device_id_type=MESH,
        )

    def copy_to(side, tile):
        if tile == 4:
            src, dst = raw, raw_in
        else:
            src, dst = mine, around.at[side, 8 - tile]
        return pltpu.make_async_remote_copy(
            src_ref=src,
            dst_ref=dst,
            send_sem=send.at[side, tile],
            recv_sem=recv.at[side, tile],
            device_id=place(side, tile),
            device_id_type=MESH,
        )

    near, far = range(1, 2 * PER_GROUP), range(2 * PER_GROUP, SLOTS)
    pl.semaphore_wait(barrier, SLOTS - 1 + 4 + len(peers))
    for slot in near:
        k_copy(slot).start()
    for slot in near:
        q_copy(slot).start()

    loads[0].wait()
    loads[1].wait()
    for head in range(SLOTS):
        cols = slice(head * HD, (head + 1) * HD)
        projected = lax.dot_general(
            v_ref[:, cols], w_ref[:, cols], (((1,), (1,)), ((), ())), preferred_element_type=F32
        )
        v_out[head] = jnp.concatenate([projected[0:HALF], projected[HALF:TOK]], axis=1).astype(BF16)
    for slot in near:
        v_copy(slot).start()
    for slot in far:
        q_copy(slot).start()
    kv[0, 0, TOK:KV_ROWS, :] = v_out[row]

    w_copies = []
    for b in range(3):
        for c in range(3):
            for a in range(3):
                w_copies.append(
                    pltpu.make_async_copy(
                        wmid_hbm.at[a, b, c],
                        wmid.at[b * 3 + c, pl.ds(a * 512, 512)],
                        w_sem.at[(b * 3 + c) * 3 + a],
                    )
                )
    for copy in w_copies:
        copy.start()

    o_ref[...] = jnp.zeros_like(o_ref)
    m_ref[...] = jnp.full_like(m_ref, NEG_FILL)
    kv_lane = lax.broadcasted_iota(jnp.int32, (HALF, HD), 1)
    ones = jnp.where(kv_lane == HD // 2, 1.0, 0.0).astype(F32)

    def first_hop(group):
        for slot in range(group * PER_GROUP, (group + 1) * PER_GROUP):
            if slot:
                k_copy(slot).wait_recv()
                v_copy(slot).wait_recv()
        for kind in (0, 1, 2, 3):
            hop_copy(kind, group).start()

    def second_hop(group):
        for kind in (0, 1, 2):
            hop_copy(kind, group).wait_recv()
        for kind in (4, 5, 6):
            hop_copy(kind, group).start()

    def from_sibling(group):
        for kind in (3, 4, 5, 6):
            hop_copy(kind, group).wait_recv()

    for copy in loads[2:]:
        copy.wait()
    first_hop(0)

    cells = [
        (
            (f // 3) * 4 + p * 2 + s,
            pl.ds((f % 3) * PLACES + i * TCOLS, TCOLS),
            pl.ds(f * 64 + (2 * i + p) * 8 + s, TCOLS, stride=2),
        )
        for f in range(FRAMES)
        for i in range(TROWS)
        for p in range(2)
        for s in range(2)
    ]
    for piece, packed_rows, tile_rows in cells:
        pieces[piece, packed_rows, :] = lat_in[tile_rows, :]
    lat_ref[...] = jnp.concatenate([pieces[piece] for piece in range(8)], axis=1)

    zero = jnp.zeros((16, 512), BF16)
    for a in range(3):
        for r in range(4):
            for c in range(4):
                lanes = (((r // 2) * 2 + c // 2) * 4 + (r % 2) * 2 + c % 2) * 16
                for pp in range(2):
                    for ss in range(2):
                        inside = 0 <= r - pp < 3 and 0 <= c - ss < 3
                        w_in[
                            a * 256 + lanes : a * 256 + lanes + 16,
                            (pp * 2 + ss) * 512 : (pp * 2 + ss + 1) * 512,
                        ] = win_ref[a, r - pp, c - ss] if inside else zero

    text_rows = tk_ref.shape[0]
    text_projected = lax.dot_general(
        tv_ref[...], w_ref[:, head_cols], (((1,), (1,)), ((), ())), preferred_element_type=F32
    )
    text_lane = lax.broadcasted_iota(jnp.int32, (text_rows, HD // 2), 1)
    text_value[...] = jnp.concatenate(
        [text_projected, jnp.where(text_lane == 0, 1.0, 0.0).astype(F32)], axis=1
    ).astype(BF16)

    def attend_text(part):
        usable = lax.broadcasted_iota(jnp.int32, (PART, text_rows), 1) < len_ref[0]
        attend(q_ref, o_ref, m_ref, part, tk_ref, text_value, usable)

    def share_of(slot):
        out = o_ref[slot * TOK : (slot + 1) * TOK, :]
        share = out[:, 0 : HD // 2] / out[:, HD // 2 : HD // 2 + 1]
        return jnp.concatenate([share[0:HALF], share[HALF:TOK]], axis=1)

    def send_shares(slots):
        for slot in slots:
            sh_out[slot] = share_of(slot).astype(BF16)
            share_copy(slot).start()

    for slot in near:
        q_copy(slot).wait_recv()
    attend_text(0)
    second_hop(0)
    first_hop(1)

    def before_1():
        from_sibling(0)
        for slot in far[:PER_GROUP]:
            q_copy(slot).wait_send()
            k_copy(slot).start()
            v_copy(slot).start()

    def before_2():
        for slot in far[PER_GROUP:]:
            q_copy(slot).wait_send()
            k_copy(slot).start()
            v_copy(slot).start()
        for slot in far:
            q_copy(slot).wait_recv()
        attend_text(1)

    def before_3():
        second_hop(1)

    def before_5():
        first_hop(2)

    def before_6():
        from_sibling(1)

    def before_7():
        first_hop(3)

    def before_8():
        second_hop(2)

    def before_10():
        from_sibling(2)
        second_hop(3)

    def before_14():
        from_sibling(3)

    def before_15():
        send_shares(reversed(far))

    steps = {
        1: before_1,
        2: before_2,
        3: before_3,
        5: before_5,
        6: before_6,
        7: before_7,
        8: before_8,
        10: before_10,
        14: before_14,
        15: before_15,
    }

    @pl.loop(0, 4 * GROUPS)
    def _(unit):
        for when, step in steps.items():
            pl.when(unit == when)(step)
        opening = (19 - unit) // 16
        closing = (unit + 2) // 16
        even = 1 - unit % 2
        chunk = opening * (unit % 2) + (1 - opening) * (unit // 2)
        usual = (1 - closing) * (1 - even) + closing * even
        part = opening * (unit // 2) + (1 - opening) * usual
        fresh = opening * (1 - unit // 2) + (1 - opening) * even
        group, side, slab = chunk // 2, chunk % 2, chunk % 2

        @pl.when(fresh == 1)
        def _():
            for member in range(4):
                for slot in range(PER_GROUP):
                    at = (member * PER_GROUP + slot) * TOK
                    block = kv.at[4 * side + member, group * PER_GROUP + slot]
                    key_ref[slab, at : at + TOK, :] = block[0:TOK, :]
                    packed = block[TOK:KV_ROWS, :].astype(F32)
                    value_ref[slab, at : at + HALF, :] = jnp.where(
                        kv_lane < HD // 2, packed, ones
                    ).astype(BF16)
                    value_ref[slab, at + HALF : at + TOK, :] = jnp.where(
                        kv_lane < HD // 2, pltpu.roll(packed, HD // 2, 1), ones
                    ).astype(BF16)

        attend(q_ref, o_ref, m_ref, part, key_ref.at[slab], value_ref.at[slab], None)

    send_shares(reversed(near))
    velocity = share_of(0)
    for slot in range(1, SLOTS):
        share_copy(slot).wait_recv()
        velocity = velocity + sh_in[slot].astype(F32)

    index = step_ref[0].astype(F32)
    advance = sigma_at(index + 1.0) - sigma_at(index)
    first = branch == 0
    raw[...] = velocity
    keep = jnp.where(first, 1.0, 0.0)
    gain = jnp.where(first, COND_GAIN, UNCOND_GAIN) * advance
    mine[...] = lat_ref[...] * keep + velocity * gain
    for side, tile in peers:
        copy_to(side, tile).start()
    for side, tile in peers:
        copy_to(side, tile).wait_recv()

    cond = jnp.where(first, raw[...], raw_in[...])
    uncond = jnp.where(first, raw_in[...], raw[...])
    guided = COND_GAIN * cond + UNCOND_GAIN * uncond
    for piece in range(8):
        pieces[piece] = guided[:, piece * 16 : (piece + 1) * 16]
    for piece, packed_rows, tile_rows in cells:
        guided_ref[tile_rows, :] = pieces[piece, packed_rows, :]
    for tile, (dr, dc) in enumerate(AROUND):
        if tile == 4:
            value = lat_ref[...] + advance * guided
        else:
            there_row, there_col = row + dr, col + dc
            there = (
                (there_row >= 0)
                & (there_row < row_count)
                & (there_col >= 0)
                & (there_col < col_count)
            )
            value = (around[0, tile] + around[1, tile]) * jnp.where(there, 1.0, 0.0)
        moved[tile * HALF : (tile + 1) * HALF, :] = value.astype(BF16)

    picked = jnp.dot(pick_ref[...], moved[...], preferred_element_type=F32)
    lane = lax.broadcasted_iota(jnp.int32, (HALF, HD), 1)
    low = lane < HD // 2
    for e in range(3):
        for g in range(2):
            at = (e * 3 + g) * HALF
            here, right = picked[at : at + HALF], picked[at + HALF : at + 2 * HALF]
            early = jnp.where(low, here, pltpu.roll(right, HD // 2, 1)).astype(BF16)
            late = jnp.where(low, pltpu.roll(here, HD // 2, 1), right).astype(BF16)
            shifted[e, g, 0:PLACES, :] = early[0:PLACES]
            shifted[e, g, PLACES : 2 * PLACES, :] = early[0:PLACES]
            shifted[e, g, 2 * PLACES : 2 * PLACES + HALF, :] = early
            shifted[e, g, 2 * PLACES + HALF : PADDED_ROWS, :] = late

    patches = jnp.concatenate(
        [
            jnp.concatenate(
                [
                    shifted[db + du, dc, a * PLACES : a * PLACES + ROWS, :]
                    for a in range(3)
                    for du in range(2)
                ],
                axis=1,
            )
            for db in range(2)
            for dc in range(2)
        ],
        axis=0,
    )

    at = lax.broadcasted_iota(jnp.int32, (ROWS, 1), 0)
    row_at, col_at = (at // TCOLS) % TROWS, at % TCOLS
    bias_in = bin_ref[...]
    for pp in range(2):
        for ss in range(2):
            kind = pp * 2 + ss
            for half in range(2):
                cols = slice(half * 256, (half + 1) * 256)
                hidden = (
                    jnp.dot(
                        patches,
                        w_in[:, kind * 512 + half * 256 : kind * 512 + (half + 1) * 256],
                        preferred_element_type=F32,
                    )
                    + bias_in[:, cols]
                )
                for db in range(2):
                    for dc in range(2):
                        shift = db * 2 + dc
                        block = hidden[shift * ROWS : (shift + 1) * ROWS]
                        if (db, dc) == (1 - pp, 1 - ss):
                            center[kind, :, cols] = block
                        y_at = row * (2 * TROWS) - 1 + 2 * (row_at + db) + pp
                        x_at = col * (2 * TCOLS) - 1 + 2 * (col_at + dc) + ss
                        inside = (
                            (y_at >= 0)
                            & (y_at < row_count * 2 * TROWS)
                            & (x_at >= 0)
                            & (x_at < col_count * 2 * TCOLS)
                        )
                        value = jnp.where(inside, block * jax.nn.sigmoid(block), 0.0).astype(BF16)
                        act[kind, shift, 0:PLACES, cols] = value[0:PLACES]
                        act[kind, shift, PLACES : 2 * PLACES, cols] = value[0:PLACES]
                        act[kind, shift, 2 * PLACES : PADDED_ROWS, cols] = value

    total = None
    for b in range(3):
        for c in range(3):
            for a in range(3):
                w_copies[(b * 3 + c) * 3 + a].wait()
            window = []
            for pi in range(2):
                for si in range(2):
                    kind = ((pi + b) % 2) * 2 + (si + c) % 2
                    shift = ((pi + b) // 2) * 2 + (si + c) // 2
                    window.append(
                        jnp.concatenate(
                            [
                                act[kind, shift, a * PLACES : a * PLACES + ROWS, :]
                                for a in range(3)
                            ],
                            axis=1,
                        )
                    )
            term = jnp.dot(
                jnp.concatenate(window, axis=0), wmid[b * 3 + c], preferred_element_type=F32
            )
            total = term if total is None else total + term
    own = pl.ds(pl.multiple_of(branch * 256, 256), 256)
    for pi in range(2):
        for si in range(2):
            phase = pi * 2 + si
            result = (
                center[(1 - pi) * 2 + (1 - si), :, own]
                + total[phase * ROWS : (phase + 1) * ROWS]
                + bmid_ref[...]
            )
            for f in range(FRAMES):
                for i in range(TROWS):
                    at = f * PLACES + i * TCOLS
                    tile_rows = pl.ds(f * 64 + (2 * i + pi) * 8 + si, TCOLS, stride=2)
                    for side in range(2):
                        ordered[side, tile_rows, :] = result[
                            at : at + TCOLS, side * 128 : (side + 1) * 128
                        ]
    for side in range(2):
        out_ref[:, side * 128 : (side + 1) * 128] = ordered[side]

    for side, tile in peers:
        copy_to(side, tile).wait_send()
    for slot in range(1, SLOTS):
        k_copy(slot).wait_send()
        v_copy(slot).wait_send()
        if slot in near:
            q_copy(slot).wait_send()
        share_copy(slot).wait_send()
    for group in range(GROUPS):
        for kind in range(7):
            hop_copy(kind, group).wait_send()


def step(
    row_count, col_count,
    queries, keys, values, out_proj, text_keys, text_values, text_lengths,
    latent_cells, step_index, w_in, b_in, w_mid, b_mid,
):
    text_rows = text_keys.shape[1]
    vmem = pl.BlockSpec(memory_space=pltpu.VMEM)
    smem = pl.BlockSpec(memory_space=pltpu.SMEM)
    hbm = pl.BlockSpec(memory_space=pltpu.HBM)
    dma = pltpu.SemaphoreType.DMA
    return pl.pallas_call(
        functools.partial(step_kernel, row_count, col_count),
        out_shape=(
            jax.ShapeDtypeStruct((4 * ROWS, 16), F32),
            jax.ShapeDtypeStruct((4 * ROWS, 256), F32),
        ),
        in_specs=[hbm] * 6 + [smem] + [hbm] * 2 + [smem] + [hbm] * 4,
        out_specs=(vmem, vmem),
        scratch_shapes=[
            pltpu.VMEM((TOK, SLOTS * HD), BF16),
            pltpu.VMEM((HD // 2, SLOTS * HD), BF16),
            pltpu.VMEM((SLOTS, HALF, HD), BF16),
            pltpu.VMEM((8, SLOTS, KV_ROWS, HD), BF16),
            pltpu.VMEM((QUERIES, HD), BF16),
            pltpu.VMEM((QUERIES, HD), F32),
            pltpu.VMEM((QUERIES, HD), F32),
            pltpu.VMEM((2, CHUNK, HD), BF16),
            pltpu.VMEM((2, CHUNK, HD), BF16),
            pltpu.VMEM((text_rows, HD), BF16),
            pltpu.VMEM((text_rows, HD), BF16),
            pltpu.VMEM((text_rows, HD), BF16),
            pltpu.VMEM((SLOTS, HALF, HD), BF16),
            pltpu.VMEM((SLOTS, HALF, HD), BF16),
            pltpu.VMEM((4 * ROWS, 16), F32),
            pltpu.VMEM((8, HALF, 16), F32),
            pltpu.VMEM((HALF, HD), F32),
            pltpu.VMEM((9 * HALF, 9 * HALF), BF16),
            pltpu.VMEM((3, 3, 3, 16, 512), BF16),
            pltpu.VMEM((1, 512), F32),
            pltpu.VMEM((1, 256), F32),
            pltpu.VMEM((HALF, HD), F32),
            pltpu.VMEM((HALF, HD), F32),
            pltpu.VMEM((HALF, HD), F32),
            pltpu.VMEM((2, 9, HALF, HD), F32),
            pltpu.VMEM((9 * HALF, HD), BF16),
            pltpu.VMEM((3, 2, PADDED_ROWS, HD), BF16),
            pltpu.VMEM((768, 2048), BF16),
            pltpu.VMEM((9, 1536, 256), BF16),
            pltpu.VMEM((4, 4, PADDED_ROWS, 512), BF16),
            pltpu.VMEM((4, ROWS, 512), F32),
            pltpu.VMEM((2, 4 * ROWS, 128), F32),
            dma((SLOTS,)), dma((SLOTS,)), dma((SLOTS,)), dma((SLOTS,)), dma((SLOTS,)), dma((SLOTS,)),
            dma((7, GROUPS)), dma((7, GROUPS)), dma((SLOTS,)), dma((SLOTS,)),
            dma((2, 9)), dma((2, 9)), dma((27,)), dma((11,)),
        ],
        compiler_params=pltpu.CompilerParams(
            collective_id=0, has_side_effects=True, vmem_limit_bytes=58 * 2**20
        ),
        name="step",
    )(
        queries, keys, values, out_proj.T, text_keys, text_values, text_lengths,
        latent_cells, jnp.asarray(pick_matrix(), BF16), step_index,
        w_in, b_in[None, :], w_mid, b_mid[None, :],
    )


def local(
    row_count,
    col_count,
    queries,
    keys,
    values,
    text_keys,
    text_values,
    text_lengths,
    step_index,
    out_proj,
    latent,
    conv_in_w,
    conv_in_b,
    conv_mid_w,
    conv_mid_b,
):
    guided, decoded = step(
        row_count, col_count,
        queries, keys, values, out_proj, text_keys, text_values, text_lengths,
        latent.reshape(-1, 16), step_index, conv_in_w, conv_in_b, conv_mid_w, conv_mid_b,
    )
    return guided.reshape(latent.shape), decoded.reshape(latent.shape[:3] + (-1,))


def solution(mesh):
    return jax.shard_map(
        functools.partial(local, mesh.shape["row"], mesh.shape["col"]),
        mesh=mesh,
        in_specs=(
            P("branch", ("row", "col"), None),
            P("branch", ("row", "col"), None),
            P("branch", ("row", "col"), None),
            P("branch", None, None),
            P("branch", None, None),
            P("branch"),
            P(),
            P(),
            P(None, "row", "col", None),
            P(),
            P(),
            P(None, None, None, None, "branch"),
            P("branch"),
        ),
        out_specs=(P(None, "row", "col", None), P(None, "row", "col", "branch")),
        check_vma=False,
    )
```

time: 120 us -> 98.1 us (0.82)
  Pallas kernels: 103 us -> 92.4 us
  local copies, waits for them, and re-layouts: 13.8 us -> 3.39 us
    pallas_call x2 -> x1, Pallas kernels: 103 us -> 92.4 us  [step(): pl.pallas_call(functools.partial(step_kernel, row_count, col_count), out_...]
    unnamed x19 -> x2, local copies, waits for them, and re-layouts: 10 us -> 3.39 us
    reshape x5 -> x0, local copies, waits for them, and re-layouts: 2.67 us -> none  [the longest x1 1.02 us: local(): decoded = decoded.reshape(2, 2, FRAMES, TROWS, TCOLS, 256).transpose(2, 3...]
where the time goes in v2:
time: 98.1 us; the launch traced here: 97.7 us
  Pallas kernels  92.4 us (94%)
  local copies, waits for them, and re-layouts  3.39 us (3%)
  between operations  1.93 us (2%)
    pallas_call x1, Pallas kernels, step(): pl.pallas_call(functools.partial(step_kernel, row_count, col_count), out_...  92.4 us
    unnamed x2, local copies, waits for them, and re-layouts  3.39 us

profile of v2, /device:TPU:1, one launch (start us, length us, event | category | flops | bytes accessed | tf_op | source)
XLA Modules:
  0.0 97.7 jit_solution(9813330386230485084)
XLA Ops:
  1.9 92.4 %step.1 = (f32[384,16]{1,0:T(8,128)}, f32[384,256]{1,0:T(8,128)}) custom-call(bf16[1,96,2048]{2,1,0:T(8,128)(2,1)} %q_hbm.1, bf16[1,96,2048]{2,1,0:T(8,128)(2,1)} %k_hbm.1, bf16[1,96,2048]{2,1,0:T(8,128)(2,1)} %v_hbm.1, bf16[64,2048]{1,0:T(8,128)(2,1)} %bitcast.7, bf16[1,256,2048]{2,1,0:T(8,128)(2,1)} %tk_hbm.1, bf16[1,256,2048]{2,1,0:T(8,128)(2,1)} %tv_hbm.1, ...), custom_call_target="tpu_custom_call" | custom-call | tf_op jit(solution)/shard_map/step/pallas_call | solution.py:589
  94.3 1.6 %copy.20 = f32[6,8,8,16]{3,2,1,0:T(8,128)} copy(f32[6,8,8,16]{3,2,1,0:T(8,128)} %bitcast.8) | data formatting | bytes 49152
  95.9 1.8 %copy.21 = f32[6,8,8,256]{3,2,1,0:T(8,128)} copy(f32[6,8,8,256]{3,2,1,0:T(8,128)} %bitcast.6) | data formatting | bytes 786432

commit v3 on v2

--- a/solution.py
+++ b/solution.py
@@ -230,8 +230,14 @@
         v_out[head] = jnp.concatenate([projected[0:HALF], projected[HALF:TOK]], axis=1).astype(BF16)
     for slot in near:
         v_copy(slot).start()
+    for slot in far[:PER_GROUP]:
+        k_copy(slot).start()
+        v_copy(slot).start()
     for slot in far:
         q_copy(slot).start()
+    for slot in far[PER_GROUP:]:
+        k_copy(slot).start()
+        v_copy(slot).start()
     kv[0, 0, TOK:KV_ROWS, :] = v_out[row]
 
     w_copies = []
@@ -274,6 +280,7 @@
     for copy in loads[2:]:
         copy.wait()
     first_hop(0)
+    first_hop(1)
 
     cells = [
         (
@@ -330,42 +337,31 @@
         q_copy(slot).wait_recv()
     attend_text(0)
     second_hop(0)
-    first_hop(1)
 
     def before_1():
         from_sibling(0)
-        for slot in far[:PER_GROUP]:
-            q_copy(slot).wait_send()
-            k_copy(slot).start()
-            v_copy(slot).start()
 
     def before_2():
-        for slot in far[PER_GROUP:]:
-            q_copy(slot).wait_send()
-            k_copy(slot).start()
-            v_copy(slot).start()
         for slot in far:
             q_copy(slot).wait_recv()
         attend_text(1)
-
-    def before_3():
         second_hop(1)
-
-    def before_5():
         first_hop(2)
+
+    def before_4():
+        first_hop(3)
 
     def before_6():
         from_sibling(1)
 
     def before_7():
-        first_hop(3)
-
-    def before_8():
         second_hop(2)
+
+    def before_9():
+        second_hop(3)
 
     def before_10():
         from_sibling(2)
-        second_hop(3)
 
     def before_14():
         from_sibling(3)
@@ -376,11 +372,10 @@
     steps = {
         1: before_1,
         2: before_2,
-        3: before_3,
-        5: before_5,
+        4: before_4,
         6: before_6,
         7: before_7,
-        8: before_8,
+        9: before_9,
         10: before_10,
         14: before_14,
         15: before_15,
@@ -568,8 +563,7 @@
     for slot in range(1, SLOTS):
         k_copy(slot).wait_send()
         v_copy(slot).wait_send()
-        if slot in near:
-            q_copy(slot).wait_send()
+        q_copy(slot).wait_send()
         share_copy(slot).wait_send()
     for group in range(GROUPS):
         for kind in range(7):

time: 98.1 us -> 91.8 us (0.936)
  Pallas kernels: 92.4 us -> 86.3 us
    pallas_call x1, Pallas kernels: 92.4 us -> 86.3 us  [step(): pl.pallas_call(functools.partial(step_kernel, row_count, col_count), out_...]
where the time goes in v3:
time: 91.8 us; the launch traced here: 91.6 us
  Pallas kernels  86.3 us (94%)
  local copies, waits for them, and re-layouts  3.39 us (4%)
  between operations  1.93 us (2%)
    pallas_call x1, Pallas kernels, step(): pl.pallas_call(functools.partial(step_kernel, row_count, col_count), out_...  86.3 us
    unnamed x2, local copies, waits for them, and re-layouts  3.39 us

profile of v3, /device:TPU:1, one launch (start us, length us, event | category | flops | bytes accessed | tf_op | source)
XLA Modules:
  0.0 91.6 jit_solution(16692396416706017338)
XLA Ops:
  1.9 86.3 %step.1 = (f32[384,16]{1,0:T(8,128)}, f32[384,256]{1,0:T(8,128)}) custom-call(bf16[1,96,2048]{2,1,0:T(8,128)(2,1)} %q_hbm.1, bf16[1,96,2048]{2,1,0:T(8,128)(2,1)} %k_hbm.1, bf16[1,96,2048]{2,1,0:T(8,128)(2,1)} %v_hbm.1, bf16[64,2048]{1,0:T(8,128)(2,1)} %bitcast.7, bf16[1,256,2048]{2,1,0:T(8,128)(2,1)} %tk_hbm.1, bf16[1,256,2048]{2,1,0:T(8,128)(2,1)} %tv_hbm.1, ...), custom_call_target="tpu_custom_call" | custom-call | tf_op jit(solution)/shard_map/step/pallas_call | solution.py:583
  88.2 1.6 %copy.20 = f32[6,8,8,16]{3,2,1,0:T(8,128)} copy(f32[6,8,8,16]{3,2,1,0:T(8,128)} %bitcast.8) | data formatting | bytes 49152
  89.8 1.8 %copy.21 = f32[6,8,8,256]{3,2,1,0:T(8,128)} copy(f32[6,8,8,256]{3,2,1,0:T(8,128)} %bitcast.6) | data formatting | bytes 786432

commit v4 on v3

--- a/solution.py
+++ b/solution.py
@@ -342,11 +342,11 @@
         from_sibling(0)
 
     def before_2():
+        second_hop(1)
+        first_hop(2)
         for slot in far:
             q_copy(slot).wait_recv()
         attend_text(1)
-        second_hop(1)
-        first_hop(2)
 
     def before_4():
         first_hop(3)
@@ -357,7 +357,7 @@
     def before_7():
         second_hop(2)
 
-    def before_9():
+    def before_8():
         second_hop(3)
 
     def before_10():
@@ -375,7 +375,7 @@
         4: before_4,
         6: before_6,
         7: before_7,
-        9: before_9,
+        8: before_8,
         10: before_10,
         14: before_14,
         15: before_15,

time: 91.8 us -> 93.2 us (1.015)
  Pallas kernels: 86.3 us -> 87.7 us
    pallas_call x1, Pallas kernels: 86.3 us -> 87.7 us  [step(): pl.pallas_call(functools.partial(step_kernel, row_count, col_count), out_...]
where the time goes in v4:
time: 93.2 us; the launch traced here: 93 us
  Pallas kernels  87.7 us (94%)
  local copies, waits for them, and re-layouts  3.39 us (4%)
  between operations  1.93 us (2%)
    pallas_call x1, Pallas kernels, step(): pl.pallas_call(functools.partial(step_kernel, row_count, col_count), out_...  87.7 us
    unnamed x2, local copies, waits for them, and re-layouts  3.39 us

profile of v4, /device:TPU:1, one launch (start us, length us, event | category | flops | bytes accessed | tf_op | source)
XLA Modules:
  0.0 93.0 jit_solution(8443996504604164523)
XLA Ops:
  1.9 87.7 %step.1 = (f32[384,16]{1,0:T(8,128)}, f32[384,256]{1,0:T(8,128)}) custom-call(bf16[1,96,2048]{2,1,0:T(8,128)(2,1)} %q_hbm.1, bf16[1,96,2048]{2,1,0:T(8,128)(2,1)} %k_hbm.1, bf16[1,96,2048]{2,1,0:T(8,128)(2,1)} %v_hbm.1, bf16[64,2048]{1,0:T(8,128)(2,1)} %bitcast.7, bf16[1,256,2048]{2,1,0:T(8,128)(2,1)} %tk_hbm.1, bf16[1,256,2048]{2,1,0:T(8,128)(2,1)} %tv_hbm.1, ...), custom_call_target="tpu_custom_call" | custom-call | tf_op jit(solution)/shard_map/step/pallas_call | solution.py:583
  89.6 1.6 %copy.20 = f32[6,8,8,16]{3,2,1,0:T(8,128)} copy(f32[6,8,8,16]{3,2,1,0:T(8,128)} %bitcast.8) | data formatting | bytes 49152
  91.2 1.8 %copy.21 = f32[6,8,8,256]{3,2,1,0:T(8,128)} copy(f32[6,8,8,256]{3,2,1,0:T(8,128)} %bitcast.6) | data formatting | bytes 786432
